TPU v7x, 32 devices: a whole 2x2x4 slice. The times are simulated.
32 devices in a mesh: groups: 2 (over x), out: 16 (over z, y, core).
Axes of the slice: x: 2, y: 2, z: 4, core: 2. Of those that a mesh axis runs over, the one named last changes fastest.
Arguments:
- stream: bfloat16 [128, 12288], P('groups', 'out'), parts along dimension 0, may hold values from -6 to 6
- norm_gain: float32 [12288], replicated, may hold values from 0.5 to 1.5
- w_query: bfloat16 [12288, 6144], P(None, 'out')
- w_keyval: bfloat16 [12288, 1024], P(None, 'out'), may hold values from -0.0546875 to 0.0546875
- w_out: bfloat16 [6144, 12288], P('out'), may hold values from -0.75 to 0.75
- lengths: int32 [128], P(('groups', 'out')), parts along dimension 0, may hold values from 1 to 512, as said below
- key_cache: bfloat16 [128, 512, 512], P(('groups', 'out')), parts along dimension 0, may hold values from -127 to 127, as said below
- value_cache: bfloat16 [128, 512, 512], P(('groups', 'out')), parts along dimension 0, may hold values from -127 to 127, as said below
- key_scales: int32 [128, 4, 4], P(('groups', 'out')), parts along dimension 0, may hold values from -8 to -6
- value_scales: int32 [128, 4, 4], P(('groups', 'out')), parts along dimension 0, may hold values from -8 to -6
Outputs:
- new_stream: bfloat16 [128, 12288], P('groups', 'out'), parts along dimension 0
There are 2 independent parts, one for each index of `groups`. A program takes and returns all parts, laid end to end along the dimension named above; an argument that names none is the same for every part. Nothing has to cross between parts.
Inputs may be any that keep to these rules, and one draw needn't show every extreme that they name: `lengths`: every row holds at least one earlier token; in every draw some row holds exactly 512. `key_cache`: whole numbers, codes of an eight-bit cache. `value_cache`: whole numbers, codes of an eight-bit cache.
All inputs are finite; a program needn't handle non-finite values.
Results may differ from a plain program's by a relative error of at most 0.024.
The roundings to bfloat16 on the way count: a program that leaves them out, or rounds other values in their place, can miss the bound.
Values may be sent and summed in bfloat16 or wider, within the bound.
A program may use at most 64 MiB of HBM per device.

v0:
```python
import functools
import math

import jax
import jax.numpy as jnp
from jax import lax
from jax.experimental import pallas as pl
from jax.experimental.pallas import tpu as pltpu
from jax.sharding import PartitionSpec as P

HQ = 48
KVH = 4
HD = 128


rope_base = 1000000.0
norm_eps = 1e-05


def rotate(vec, position):
    half = vec.shape[-1] // 2
    index = jnp.arange(half, dtype=jnp.float32)
    freq = jnp.exp(index * (-2.0 * math.log(rope_base) / vec.shape[-1]))
    angle = position * freq
    cosine = jnp.cos(angle)
    sine = jnp.sin(angle)
    first = vec[..., :half]
    second = vec[..., half:]
    return jnp.concatenate(
        [first * cosine - second * sine, second * cosine + first * sine], axis=-1
    )


def dequant(cache, scales):
    rows, span, width = cache.shape
    blocks = scales.shape[1]
    factor = jnp.exp2(scales.astype(jnp.float32)).astype(jnp.bfloat16)
    shaped = cache.reshape(rows, blocks, span // blocks, KVH, width // KVH)
    return (shaped * factor[:, :, None, :, None]).reshape(rows, span, KVH, width // KVH)


def plain_device(
    stream,
    norm_gain,
    w_query,
    w_keyval,
    w_out,
    lengths,
    key_cache,
    value_cache,
    key_scales,
    value_scales,
):
    local_rows = lengths.shape[0]
    xf = stream.astype(jnp.float32)
    whole = lax.all_gather(stream, "out", axis=1, tiled=True).astype(jnp.float32)
    meansq = jnp.mean(whole * whole, axis=-1, keepdims=True)
    normed = (whole * lax.rsqrt(meansq + norm_eps) * norm_gain).astype(jnp.bfloat16)
    q_local = jnp.dot(normed, w_query, preferred_element_type=jnp.float32).astype(jnp.bfloat16)
    kv_local = jnp.dot(normed, w_keyval, preferred_element_type=jnp.float32).astype(jnp.bfloat16)
    q_rows, kv_rows = (
        lax.all_to_all(q_local, "out", split_axis=0, concat_axis=1, tiled=True),
        lax.all_to_all(kv_local, "out", split_axis=0, concat_axis=1, tiled=True),
    )
    position = lengths.astype(jnp.float32)[:, None, None]
    rotated = rotate(q_rows.astype(jnp.float32).reshape(local_rows, HQ, HD), position).astype(
        jnp.bfloat16
    )
    rotated = rotated.reshape(local_rows, KVH, HQ // KVH, HD)
    new_key = rotate(
        kv_rows[:, : KVH * HD].astype(jnp.float32).reshape(local_rows, KVH, HD), position
    ).astype(jnp.bfloat16)
    new_value = kv_rows[:, KVH * HD :].reshape(local_rows, KVH, HD)
    factor = HD ** (-0.5)
    own = jnp.einsum("rkgd,rkd->rkg", rotated, new_key, preferred_element_type=jnp.float32) * factor
    span = key_cache.shape[1]
    scores = (
        jnp.einsum(
            "rkgd,rjkd->rkgj",
            rotated,
            dequant(key_cache, key_scales),
            preferred_element_type=jnp.float32,
        )
        * factor
    )
    valid = jnp.arange(span, dtype=jnp.int32)[None, :] < lengths[:, None]
    scores = jnp.where(valid[:, None, None, :], scores, -jnp.inf)
    top = jnp.maximum(jnp.max(scores, axis=-1), own)
    weights = jnp.exp(scores - top[..., None])
    own_weight = jnp.exp(own - top)
    total = jnp.sum(weights, axis=-1) + own_weight
    own_rounded = lax.optimization_barrier(own_weight.astype(jnp.bfloat16)).astype(jnp.float32)
    summed = jnp.einsum(
        "rkgj,rjkd->rkgd",
        weights.astype(jnp.bfloat16),
        dequant(value_cache, value_scales),
        preferred_element_type=jnp.float32,
    )
    summed = summed + own_rounded[..., None] * new_value.astype(jnp.float32)[:, :, None, :]
    attended = (summed / total[..., None]).astype(jnp.bfloat16).reshape(local_rows, HQ * HD)
    heads = lax.all_to_all(attended, "out", split_axis=1, concat_axis=0, tiled=True)
    partial_terms = jnp.dot(heads, w_out, preferred_element_type=jnp.float32)
    projected = lax.psum_scatter(partial_terms, "out", scatter_dimension=1, tiled=True)
    return (xf + projected).astype(jnp.bfloat16)


MESH = pl.DeviceIdType.MESH
F32 = jnp.float32
BF16 = jnp.bfloat16
CONTRACT_LAST = (((1,), (1,)), ((), ()))


def fused_kernel(
    n, rows, width, local_rows, span,
    len_ref, ks_ref, vs_ref,
    x_hbm, gain_hbm, wq_hbm, wkv_hbm, wo_hbm, kc_hbm, vc_hbm,
    out_ref,
    x_ref, gain_ref, cos_ref, sin_ref, kfac, vfac, wq, wkv, wo, kc, vc, xbuf, ssend, sbuf, accq, pk, qsend, qbuf, asend, abuf, heads,
    core_sb, core_rb, y_sb, y_rb, z_sb, up_rb, dn_rb, heads_sum,
    wq_sem, wo_sem, w_sem,
    ag_recv, ag_up, ag_dn, ag_y, ag_core,
    ss_send, ss_recv, q_send, q_recv, a_send, a_recv,
    core_send, core_recv, y_send, y_recv, z_send, up_recv, dn_recv,
):
    line = n // 4
    qcols = heads.shape[1]
    kv_cols = wkv_hbm.shape[0]
    own_heads = qcols // HD
    tile = qbuf.shape[1]
    per_head = n // KVH
    qrows = per_head * tile
    me = lax.axis_index("out")
    grp = lax.axis_index("groups")
    a = me // 4
    b = (me // 2) % 2
    c = me % 2

    def at(pos, bb, cc):
        return (pos * 2 + bb) * 2 + cc

    up, down = at(a + 1, b, c), at(a - 1, b, c)
    ypeer, cpeer = at(a, 1 - b, c), at(a, b, 1 - c)
    low, high = a, line - 1 - a
    least = jnp.minimum(low, high)

    def ranked(m):
        d = (m + 1) // 2
        near = jnp.where(m % 2 == 1, a - d, a + d)
        far = jnp.where(high > low, a + (m - least), a - (m - least))
        return jnp.where(m <= 2 * least, near, far)

    def remote(src, dst, ssem, rsem, to):
        return pltpu.make_async_remote_copy(
            src_ref=src, dst_ref=dst, send_sem=ssem, recv_sem=rsem,
            device_id=(grp, to), device_id_type=MESH,
        )

    def wq_copy(i):
        at_rows = pl.ds(pl.multiple_of(i * width, width), width)
        return pltpu.make_async_copy(wq_hbm.at[at_rows], wq.at[at_rows, pl.ds(0, qcols)], wq_sem.at[i])

    wo_parts = wo_sem.shape[0]
    wo_rows = wo.shape[0] // wo_parts

    def wo_copy(i):
        at_rows = pl.ds(i * wo_rows, wo_rows)
        return pltpu.make_async_copy(wo_hbm.at[at_rows], wo.at[at_rows], wo_sem.at[i])

    wkv_copy = pltpu.make_async_copy(wkv_hbm, wkv.at[pl.ds(0, kv_cols)], w_sem.at[0])
    kc_copy = pltpu.make_async_copy(kc_hbm, kc, w_sem.at[1])
    vc_copy = pltpu.make_async_copy(vc_hbm, vc, w_sem.at[2])

    x_copy = pltpu.make_async_copy(x_hbm, x_ref, w_sem.at[3])
    gain_copy = pltpu.make_async_copy(gain_hbm, gain_ref, w_sem.at[4])
    x_copy.start()
    gain_copy.start()

    barrier = pltpu.get_barrier_semaphore()

    def others(body):
        def step(i, carry):
            body(lax.rem(me + i, n))
            return carry
        lax.fori_loop(1, n, step, 0)

    others(lambda o: pl.semaphore_signal(barrier, inc=1, device_id=(grp, o), device_id_type=MESH))

    wkv_copy.start()
    if kv_cols < HD:
        wkv[kv_cols:, :] = jnp.zeros((HD - kv_cols, n * width), BF16)

    def start_wq(m, carry):
        pos = ranked(m)
        for bb, cc in ((b, c), (b, 1 - c), (1 - b, c), (1 - b, 1 - c)):
            wq_copy(at(pos, bb, cc)).start()
        return carry
    lax.fori_loop(0, line, start_wq, 0)

    x_copy.wait()
    xbuf[me] = x_ref[...]
    xf = x_ref[...].astype(F32)
    square = jnp.sum(xf * xf, axis=1, keepdims=True)
    spread = jnp.transpose(jnp.broadcast_to(square, (rows, 128)))
    ssend[...] = jnp.zeros_like(ssend)
    ssend[:, 0:rows] = spread[0:8, :]
    sbuf[me] = ssend[...]
    accq[...] = jnp.zeros_like(accq)

    pl.semaphore_wait(barrier, n - 1)

    half_rows = rows // 2

    def ag_copy(block, h, ssem, to):
        part = xbuf.at[block, pl.ds(h * half_rows, half_rows)]
        return remote(part, part, ssem, ag_recv.at[2 * block + h], to)

    def ag_wait(block, h):
        ag_copy(block, h, ag_core.at[0], cpeer).wait_recv()

    def spread_line(pos, h):
        block = at(pos, b, c)

        @pl.when((pos <= a) & (a < line - 1))
        def _():
            ag_copy(block, h, ag_up.at[2 * pos + h], up).start()

        @pl.when((pos >= a) & (a > 0))
        def _():
            ag_copy(block, h, ag_dn.at[2 * pos + h], down).start()

        ag_copy(block, h, ag_y.at[2 * pos + h], ypeer).start()
        ag_copy(block, h, ag_core.at[2 * pos + h], cpeer).start()

    def ss_copy(o, slot):
        return remote(ssend, sbuf.at[slot], ss_send.at[o], ss_recv.at[slot], o)

    others(lambda o: ss_copy(o, me).start())
    for h in range(2):
        spread_line(a, h)
    ridx = lax.broadcasted_iota(jnp.int32, (qrows, 128), 0) % local_rows
    pick = lax.broadcasted_iota(jnp.int32, (qrows, tile), 0) % local_rows
    pick = pick + own_heads * local_rows == lax.broadcasted_iota(jnp.int32, (qrows, tile), 1)
    pick = pick.astype(F32).astype(BF16)
    blocks = span // 128
    few = lax.broadcasted_iota(jnp.int32, (8, 128), 0) % local_rows
    lane8 = lax.broadcasted_iota(jnp.int32, (8, 128), 1)

    def by_row(values):
        res = jnp.full((8, 128), values[0])
        for r in range(1, local_rows):
            res = jnp.where(few == r, values[r], res)
        return res

    def tall(v):
        return jnp.concatenate([v] * (qrows // 8), axis=0)

    limit8 = by_row([len_ref[r] for r in range(local_rows)])
    freq = jnp.exp((lane8 % (HD // 2)).astype(F32) * (-2.0 * math.log(rope_base) / HD))
    angle = limit8.astype(F32) * freq
    cos_ref[...] = jnp.cos(angle)
    sin_ref[...] = jnp.where(lane8 < HD // 2, -1.0, 1.0) * jnp.sin(angle)
    for k in range(KVH):
        for u in range(blocks):
            for ref, table in ((ks_ref, kfac), (vs_ref, vfac)):
                power = by_row([ref[r, u, k] for r in range(local_rows)]).astype(F32)
                table[k * blocks + u] = jnp.exp2(power).astype(BF16).astype(F32)

    wkv_copy.wait()

    def turn(i, carry):
        start = pl.multiple_of(i * width, width)
        turned = jnp.transpose(wkv[:, pl.ds(start, width)].astype(F32)).astype(BF16)
        wq[pl.ds(start, width), qcols:] = turned
        return carry
    lax.fori_loop(0, n, turn, 0)
    others(lambda o: ss_copy(o, o).wait_recv())
    total_sq = jnp.sum(sbuf[...], axis=0)[0:1, :]
    column = jnp.transpose(jnp.broadcast_to(total_sq, (128, 128)))[0:rows, 0:1]
    scale = lax.rsqrt(column * (1.0 / (n * width)) + norm_eps)
    gain_copy.wait()

    def project(block):
        wq_copy(block).wait()
        start = pl.multiple_of(block * width, width)
        normed = (xbuf[block].astype(F32) * scale * gain_ref[:, pl.ds(start, width)]).astype(BF16)
        accq[...] += jnp.dot(normed, wq[pl.ds(start, width), :], preferred_element_type=F32)

    def take_line(m, h):
        @pl.when(m < line)
        def _():
            pos = ranked(m)
            ag_wait(at(pos, b, c), h)
            spread_line(pos, h)

    def take_pair(m, h):
        pos = ranked(m)
        block = at(pos, 1 - b, c)
        ag_wait(block, h)
        ag_copy(block, h, ag_core.at[2 * (line + pos) + h], cpeer).start()

    project(me)

    def gather_step(m, carry):
        take_line(m, 0)
        take_pair(m - 1, 0)
        cblock = at(ranked(m - 1), b, 1 - c)
        for h in range(2):
            ag_wait(cblock, h)
        project(cblock)
        take_line(m, 1)
        take_pair(m - 1, 1)
        project(at(ranked(m - 1), 1 - b, c))

        @pl.when(m < line)
        def _():
            project(at(ranked(m), b, c))

        @pl.when(m > 1)
        def _():
            block = at(ranked(m - 2), 1 - b, 1 - c)
            for h in range(2):
                ag_wait(block, h)
            project(block)

        @pl.when(m == 1)
        def _():
            kc_copy.start()
            vc_copy.start()
            for i in range(wo_parts):
                wo_copy(i).start()
        return carry
    lax.fori_loop(1, line + 1, gather_step, 0)
    last = at(ranked(line - 1), 1 - b, 1 - c)
    for h in range(2):
        ag_wait(last, h)
    project(last)

    pk[...] = jnp.zeros_like(pk)
    q_all = accq[...]
    kv_all = q_all[:, qcols:qcols + kv_cols]
    for j in range(n):
        mine = slice(j * local_rows, (j + 1) * local_rows)
        for g in range(own_heads):
            pk[j, g * local_rows:(g + 1) * local_rows, :] = q_all[mine, g * HD:(g + 1) * HD]
        pk[j, own_heads * local_rows:tile, 0:kv_cols] = kv_all[mine, :]
    qsend[...] = pk[...].astype(BF16)

    def q_copy(o, slot):
        return remote(qsend.at[o], qbuf.at[slot], q_send.at[o], q_recv.at[slot], o)

    others(lambda o: q_copy(o, me).start())
    qbuf[me] = qsend[me]

    limit = tall(limit8)
    lane = lax.broadcasted_iota(jnp.int32, (qrows, 128), 1)
    cosine, sine = tall(cos_ref[...]), tall(sin_ref[...])

    def rotated(v):
        return (v * cosine + pltpu.roll(v, HD // 2, 1) * sine).astype(BF16)

    kc_copy.wait()
    vc_copy.wait()
    others(lambda o: q_copy(o, o).wait_recv())

    pieces = HD // kv_cols
    factor = HD ** (-0.5)

    def new_head(first):
        res = None
        for p in range(pieces):
            part = jnp.dot(pick, qbuf[first + p], preferred_element_type=F32)
            part = part if p == 0 else pltpu.roll(part, p * kv_cols, 1)
            res = part if res is None else res + part
        return res

    for k in range(KVH):
        at_k = slice(k * HD, (k + 1) * HD)
        query = rotated(qbuf[k * per_head:(k + 1) * per_head].astype(F32).reshape(qrows, HD))
        new_key = rotated(new_head(k * pieces)).astype(F32)
        new_value = new_head((KVH + k) * pieces)
        own = jnp.sum(query.astype(F32) * new_key, axis=1, keepdims=True) * factor
        score = None
        for r in range(local_rows):
            one = lax.dot_general(query, kc[r, :, at_k], CONTRACT_LAST, preferred_element_type=F32)
            cut = [one[:, 128 * u:128 * (u + 1)] for u in range(blocks)]
            score = cut if r == 0 else [jnp.where(ridx == r, x, y) for x, y in zip(cut, score)]
        highest = None
        for u in range(blocks):
            scales = tall(kfac[k * blocks + u])
            score[u] = jnp.where(lane + 128 * u < limit, score[u] * scales * factor, -jnp.inf)
            highest = score[u] if u == 0 else jnp.maximum(highest, score[u])
        top = jnp.maximum(own, jnp.max(highest, axis=1, keepdims=True))
        own_weight = jnp.exp(own - top)
        added = None
        weights = []
        for u in range(blocks):
            weight = jnp.exp(score[u] - top)
            added = weight if u == 0 else added + weight
            scales = tall(vfac[k * blocks + u])
            weights.append((weight.astype(BF16).astype(F32) * scales).astype(BF16))
        total = own_weight + jnp.sum(added, axis=1, keepdims=True)
        weights = jnp.concatenate(weights, axis=1)
        summed = None
        for r in range(local_rows):
            one = jnp.dot(weights, vc[r, :, at_k], preferred_element_type=F32)
            summed = one if r == 0 else jnp.where(ridx == r, one, summed)
        summed = summed + own_weight.astype(BF16).astype(F32) * new_value
        result = (summed / total).astype(BF16)
        for s in range(per_head):
            asend[k * per_head + s] = result[s * tile:(s + 1) * tile, :]

    def a_copy(o, slot):
        return remote(asend.at[o], abuf.at[slot], a_send.at[o], a_recv.at[slot], o)

    others(lambda o: a_copy(o, me).start())
    abuf[me] = asend[me]
    for i in range(wo_parts):
        wo_copy(i).wait()
    others(lambda o: a_copy(o, o).wait_recv())
    pk[...] = abuf[...].astype(F32)
    for j in range(n):
        for g in range(own_heads):
            heads[j * local_rows:(j + 1) * local_rows, g * HD:(g + 1) * HD] = (
                pk[j, g * local_rows:(g + 1) * local_rows, :]
            )
    attended = heads[...].astype(BF16)

    def partial(block):
        start = pl.multiple_of(block * width, width)
        return jnp.dot(attended, wo[:, pl.ds(start, width)], preferred_element_type=F32)

    def core_copy(slot):
        return remote(core_sb.at[slot], core_rb.at[slot], core_send.at[slot], core_recv.at[slot], cpeer)

    def half_of(ref, pos, h):
        return ref.at[pos, pl.ds(h * half_rows, half_rows)]

    def y_copy(pos, h):
        i = 2 * pos + h
        return remote(half_of(y_sb, pos, h), half_of(y_rb, pos, h), y_send.at[i], y_recv.at[i], ypeer)

    def up_copy(pos, h):
        i = 2 * pos + h
        return remote(half_of(z_sb, pos, h), half_of(up_rb, pos, h), z_send.at[i], up_recv.at[i], up)

    def dn_copy(pos, h):
        i = 2 * pos + h
        return remote(half_of(z_sb, pos, h), half_of(dn_rb, pos, h), z_send.at[i], dn_recv.at[i], down)

    def to_core_far(pos):
        core_sb[line + pos] = partial(at(pos, 1 - b, 1 - c)).astype(BF16)
        core_copy(line + pos).start()

    def to_pair(pos):
        term = partial(at(pos, 1 - b, c))
        core_copy(line + pos).wait_recv()
        y_sb[pos] = (term + core_rb[line + pos].astype(F32)).astype(BF16)
        for h in range(2):
            y_copy(pos, h).start()

    def to_core_near(pos):
        core_sb[pos] = partial(at(pos, b, 1 - c)).astype(BF16)
        core_copy(pos).start()

    def to_line(pos):
        term = partial(at(pos, b, c))
        core_copy(pos).wait_recv()
        heads_sum[...] = term + core_rb[pos].astype(F32)
        for h in range(2):
            part = pl.ds(h * half_rows, half_rows)
            y_copy(pos, h).wait_recv()
            heads_sum[part] += y_rb[pos, part].astype(F32)

            @pl.when((pos >= a) & (a > 0))
            def _():
                up_copy(pos, h).wait_recv()
                heads_sum[part] += up_rb[pos, part].astype(F32)

            @pl.when((pos <= a) & (a < line - 1))
            def _():
                dn_copy(pos, h).wait_recv()
                heads_sum[part] += dn_rb[pos, part].astype(F32)

            @pl.when(pos > a)
            def _():
                z_sb[pos, part] = heads_sum[part].astype(BF16)
                up_copy(pos, h).start()

            @pl.when(pos < a)
            def _():
                z_sb[pos, part] = heads_sum[part].astype(BF16)
                dn_copy(pos, h).start()

            @pl.when(pos == a)
            def _():
                out_ref[part] = (x_ref[part].astype(F32) + heads_sum[part]).astype(BF16)

    def far(m):
        return ranked(line - 1 - m)

    to_core_far(far(0))

    def pair_step(m, carry):
        @pl.when(m + 1 < line)
        def _():
            to_core_far(far(m + 1))

        to_pair(far(m))
        return carry
    lax.fori_loop(0, line, pair_step, 0)

    to_core_near(far(0))

    def sum_step(m, carry):
        @pl.when(m + 1 < line)
        def _():
            to_core_near(far(m + 1))

        to_line(far(m))
        return carry
    lax.fori_loop(0, line, sum_step, 0)

    def sent_gather(i, carry):
        pos, h = i // 2, i % 2
        block = at(pos, b, c)

        @pl.when((pos <= a) & (a < line - 1))
        def _():
            ag_copy(block, h, ag_up.at[2 * pos + h], up).wait_send()

        @pl.when((pos >= a) & (a > 0))
        def _():
            ag_copy(block, h, ag_dn.at[2 * pos + h], down).wait_send()

        ag_copy(block, h, ag_y.at[2 * pos + h], ypeer).wait_send()
        ag_copy(block, h, ag_core.at[2 * pos + h], cpeer).wait_send()
        ag_copy(at(pos, 1 - b, c), h, ag_core.at[2 * (line + pos) + h], cpeer).wait_send()
        y_copy(pos, h).wait_send()

        @pl.when(pos > a)
        def _():
            up_copy(pos, h).wait_send()

        @pl.when(pos < a)
        def _():
            dn_copy(pos, h).wait_send()
        return carry
    lax.fori_loop(0, 2 * line, sent_gather, 0)

    def sent(pos, carry):
        core_copy(pos).wait_send()
        core_copy(line + pos).wait_send()
        return carry
    lax.fori_loop(0, line, sent, 0)

    def sent_others(o):
        ss_copy(o, o).wait_send()
        q_copy(o, o).wait_send()
        a_copy(o, o).wait_send()
    others(sent_others)


def fused_device(
    n, stream, norm_gain, w_query, w_keyval, w_out, lengths, key_cache, value_cache,
    key_scales, value_scales,
):
    rows, width = stream.shape
    local_rows = lengths.shape[0]
    span = key_cache.shape[1]
    line = n // 4
    qcols = w_query.shape[1]
    tile = (qcols // HD + 1) * local_rows
    vmem = pl.BlockSpec(memory_space=pltpu.VMEM)
    smem = pl.BlockSpec(memory_space=pltpu.SMEM)
    hbm = pl.BlockSpec(memory_space=pl.ANY)
    block = (rows, width)
    dma = pltpu.SemaphoreType.DMA
    return pl.pallas_call(
        functools.partial(fused_kernel, n, rows, width, local_rows, span),
        out_shape=jax.ShapeDtypeStruct(block, BF16),
        in_specs=[smem] * 3 + [hbm] * 7,
        out_specs=vmem,
        scratch_shapes=[
            pltpu.VMEM(block, BF16),
            pltpu.VMEM((1, n * width), F32),
            pltpu.VMEM((8, HD), F32),
            pltpu.VMEM((8, HD), F32),
            pltpu.VMEM((KVH * (span // 128), 8, 128), F32),
            pltpu.VMEM((KVH * (span // 128), 8, 128), F32),
            pltpu.VMEM((n * width, qcols + HD), BF16),
            pltpu.VMEM((HD, n * width), BF16),
            pltpu.VMEM(w_out.shape, BF16),
            pltpu.VMEM(key_cache.shape, BF16),
            pltpu.VMEM(value_cache.shape, BF16),
            pltpu.VMEM((n,) + block, BF16),
            pltpu.VMEM((8, 128), F32),
            pltpu.VMEM((n, 8, 128), F32),
            pltpu.VMEM((rows, qcols + HD), F32),
            pltpu.VMEM((n, tile, HD), F32),
            pltpu.VMEM((n, tile, HD), BF16),
            pltpu.VMEM((n, tile, HD), BF16),
            pltpu.VMEM((n, tile, HD), BF16),
            pltpu.VMEM((n, tile, HD), BF16),
            pltpu.VMEM((rows, qcols), F32),
            pltpu.VMEM((2 * line,) + block, BF16),
            pltpu.VMEM((2 * line,) + block, BF16),
            pltpu.VMEM((line,) + block, BF16),
            pltpu.VMEM((line,) + block, BF16),
            pltpu.VMEM((line,) + block, BF16),
            pltpu.VMEM((line,) + block, BF16),
            pltpu.VMEM((line,) + block, BF16),
            pltpu.VMEM(block, F32),
            dma((n,)), dma((4,)), dma((5,)),
            dma((2 * n,)), dma((2 * line,)), dma((2 * line,)), dma((2 * line,)), dma((4 * line,)),
            dma((n,)), dma((n,)), dma((n,)), dma((n,)), dma((n,)), dma((n,)),
            dma((2 * line,)), dma((2 * line,)), dma((2 * line,)), dma((2 * line,)), dma((2 * line,)),
            dma((2 * line,)), dma((2 * line,)),
        ],
        compiler_params=pltpu.CompilerParams(
            collective_id=0, has_side_effects=True, vmem_limit_bytes=62 * 2**20
        ),
        cost_estimate=pl.CostEstimate(
            flops=4 * rows * w_query.size, bytes_accessed=4 * w_query.size, transcendentals=0
        ),
    )(
        lengths, key_scales, value_scales, stream, norm_gain.reshape(1, -1),
        w_query, w_keyval.T, w_out, key_cache, value_cache,
    )


def per_device(n, *args):
    stream, _, w_query, w_keyval, _, lengths, key_cache, *_ = args
    rows, width = stream.shape
    local_rows = lengths.shape[0]
    qcols, kv_cols = w_query.shape[1], w_keyval.shape[1]
    tiles = (
        n % 4 == 0 and n >= 8 and n % KVH == 0 and width % 128 == 0 and qcols % HD == 0
        and HD % kv_cols == 0 and rows % 32 == 0 and rows <= 128
        and 8 % local_rows == 0
        and (qcols // HD + 1) * local_rows % 16 == 0
        and key_cache.shape[1] // 128 == args[8].shape[1]
    )
    return fused_device(n, *args) if tiles else plain_device(*args)


def solution(mesh):
    return jax.shard_map(
        functools.partial(per_device, mesh.shape["out"]),
        mesh=mesh,
        in_specs=(
            P("groups", "out"),
            P(),
            P(None, "out"),
            P(None, "out"),
            P("out", None),
            P(("groups", "out")),
            P(("groups", "out"), None, None),
            P(("groups", "out"), None, None),
            P(("groups", "out"), None, None),
            P(("groups", "out"), None, None),
        ),
        out_specs=P("groups", "out"),
        check_vma=False,
    )
```

profile of v0, /device:TPU:0, one launch (start us, length us, event | category | flops | bytes accessed | tf_op | source)
XLA Modules:
  0.0 57.1 jit_solution(13340328614615886892)
XLA Ops:
  0.0 55.5 %shard_map.100 = bf16[64,768]{1,0:T(8,128)(2,1)} custom-call(s32[4]{0:T(128)} %len_ref.1, s32[4,4,4]{2,1,0:T(4,128)} %ks_ref.1, s32[4,4,4]{2,1,0:T(4,128)} %vs_ref.1, bf16[64,768]{1,0:T(8,128)(2,1)} %x_hbm.1, f32[1,12288]{1,0:T(1,128)} %bitcast.3, bf16[12288,384]{1,0:T(8,128)(2,1)} %wq_hbm.1, bf16[64,12288]{1,0:T(8,128)(2,1)} %bitcast.2, ...), custom_call_target="tpu_custom_call" | custom-call | flops 1207959552 | bytes 18874368 | tf_op jit(solution)/shard_map/pallas_call | solution.py:578
  55.5 1.5 %copy.12 = bf16[64,768]{1,0:T(8,128)(2,1)} copy(bf16[64,768]{1,0:T(8,128)(2,1)} %shard_map.100) | data formatting | bytes 196608
where the time goes:
time: 57.3 us; the launch traced here: 57.1 us
  Pallas kernels  55.5 us (97%)
  local copies, waits for them, and re-layouts  1.54 us (3%)
    pallas_call x1, Pallas kernels, fused_device(): pl.pallas_call(functools.partial(fused_kernel, n, rows, width, local_rows...  55.5 us
    unnamed x1, local copies, waits for them, and re-layouts  1.54 us

commit v1 on v0

--- a/solution.py
+++ b/solution.py
@@ -265,6 +265,25 @@
                 power = by_row([ref[r, u, k] for r in range(local_rows)]).astype(F32)
                 table[k * blocks + u] = jnp.exp2(power).astype(BF16).astype(F32)
 
+    def take_line(m, h):
+        @pl.when(m < line)
+        def _():
+            pos = ranked(m)
+            ag_wait(at(pos, b, c), h)
+            spread_line(pos, h)
+
+    def take_pair(m, h):
+        @pl.when(m < line)
+        def _():
+            pos = ranked(m)
+            block = at(pos, 1 - b, c)
+            ag_wait(block, h)
+            ag_copy(block, h, ag_core.at[2 * (line + pos) + h], cpeer).start()
+
+    for h in range(2):
+        take_line(1, h)
+        take_pair(0, h)
+
     wkv_copy.wait()
 
     def turn(i, carry):
@@ -285,35 +304,18 @@
         normed = (xbuf[block].astype(F32) * scale * gain_ref[:, pl.ds(start, width)]).astype(BF16)
         accq[...] += jnp.dot(normed, wq[pl.ds(start, width), :], preferred_element_type=F32)
 
-    def take_line(m, h):
-        @pl.when(m < line)
-        def _():
-            pos = ranked(m)
-            ag_wait(at(pos, b, c), h)
-            spread_line(pos, h)
-
-    def take_pair(m, h):
-        pos = ranked(m)
-        block = at(pos, 1 - b, c)
-        ag_wait(block, h)
-        ag_copy(block, h, ag_core.at[2 * (line + pos) + h], cpeer).start()
-
-    project(me)
-
     def gather_step(m, carry):
-        take_line(m, 0)
-        take_pair(m - 1, 0)
-        cblock = at(ranked(m - 1), b, 1 - c)
+        prev = ranked(m - 1)
+        project(at(prev, b, c))
+        take_line(m + 1, 0)
+        take_pair(m, 0)
+        cblock = at(prev, b, 1 - c)
         for h in range(2):
             ag_wait(cblock, h)
         project(cblock)
-        take_line(m, 1)
-        take_pair(m - 1, 1)
-        project(at(ranked(m - 1), 1 - b, c))
-
-        @pl.when(m < line)
-        def _():
-            project(at(ranked(m), b, c))
+        take_line(m + 1, 1)
+        take_pair(m, 1)
+        project(at(prev, 1 - b, c))
 
         @pl.when(m > 1)
         def _():
@@ -350,6 +352,25 @@
 
     others(lambda o: q_copy(o, me).start())
     qbuf[me] = qsend[me]
+    def sent_gather(i, carry):
+        pos, h = i // 2, i % 2
+        block = at(pos, b, c)
+
+        @pl.when((pos <= a) & (a < line - 1))
+        def _():
+            ag_copy(block, h, ag_up.at[2 * pos + h], up).wait_send()
+
+        @pl.when((pos >= a) & (a > 0))
+        def _():
+            ag_copy(block, h, ag_dn.at[2 * pos + h], down).wait_send()
+
+        ag_copy(block, h, ag_y.at[2 * pos + h], ypeer).wait_send()
+        ag_copy(block, h, ag_core.at[2 * pos + h], cpeer).wait_send()
+        ag_copy(at(pos, 1 - b, c), h, ag_core.at[2 * (line + pos) + h], cpeer).wait_send()
+        return carry
+    lax.fori_loop(0, 2 * line, sent_gather, 0)
+    others(lambda o: ss_copy(o, o).wait_send())
+
 
     limit = tall(limit8)
     lane = lax.broadcasted_iota(jnp.int32, (qrows, 128), 1)
@@ -414,6 +435,7 @@
 
     others(lambda o: a_copy(o, me).start())
     abuf[me] = asend[me]
+    others(lambda o: q_copy(o, o).wait_send())
     for i in range(wo_parts):
         wo_copy(i).wait()
     others(lambda o: a_copy(o, o).wait_recv())
@@ -510,6 +532,7 @@
     lax.fori_loop(0, line, pair_step, 0)
 
     to_core_near(far(0))
+    others(lambda o: a_copy(o, o).wait_send())
 
     def sum_step(m, carry):
         @pl.when(m + 1 < line)
@@ -520,21 +543,8 @@
         return carry
     lax.fori_loop(0, line, sum_step, 0)
 
-    def sent_gather(i, carry):
+    def sent_sums(i, carry):
         pos, h = i // 2, i % 2
-        block = at(pos, b, c)
-
-        @pl.when((pos <= a) & (a < line - 1))
-        def _():
-            ag_copy(block, h, ag_up.at[2 * pos + h], up).wait_send()
-
-        @pl.when((pos >= a) & (a > 0))
-        def _():
-            ag_copy(block, h, ag_dn.at[2 * pos + h], down).wait_send()
-
-        ag_copy(block, h, ag_y.at[2 * pos + h], ypeer).wait_send()
-        ag_copy(block, h, ag_core.at[2 * pos + h], cpeer).wait_send()
-        ag_copy(at(pos, 1 - b, c), h, ag_core.at[2 * (line + pos) + h], cpeer).wait_send()
         y_copy(pos, h).wait_send()
 
         @pl.when(pos > a)
@@ -545,19 +555,13 @@
         def _():
             dn_copy(pos, h).wait_send()
         return carry
-    lax.fori_loop(0, 2 * line, sent_gather, 0)
+    lax.fori_loop(0, 2 * line, sent_sums, 0)
 
     def sent(pos, carry):
         core_copy(pos).wait_send()
         core_copy(line + pos).wait_send()
         return carry
     lax.fori_loop(0, line, sent, 0)
-
-    def sent_others(o):
-        ss_copy(o, o).wait_send()
-        q_copy(o, o).wait_send()
-        a_copy(o, o).wait_send()
-    others(sent_others)
 
 
 def fused_device(

time: 57.3 us -> 57.8 us (level)
  no operation moved by 1% of the time
where the time goes in v1:
time: 57.8 us; the launch traced here: 57.6 us
  Pallas kernels  56 us (97%)
  local copies, waits for them, and re-layouts  1.54 us (3%)
    pallas_call x1, Pallas kernels, fused_device(): pl.pallas_call(functools.partial(fused_kernel, n, rows, width, local_rows...  56 us
    unnamed x1, local copies, waits for them, and re-layouts  1.54 us

profile of v1, /device:TPU:0, one launch (start us, length us, event | category | flops | bytes accessed | tf_op | source)
XLA Modules:
  0.0 57.6 jit_solution(6867574792785265900)
XLA Ops:
  0.0 56.0 %shard_map.100 = bf16[64,768]{1,0:T(8,128)(2,1)} custom-call(s32[4]{0:T(128)} %len_ref.1, s32[4,4,4]{2,1,0:T(4,128)} %ks_ref.1, s32[4,4,4]{2,1,0:T(4,128)} %vs_ref.1, bf16[64,768]{1,0:T(8,128)(2,1)} %x_hbm.1, f32[1,12288]{1,0:T(1,128)} %bitcast.3, bf16[12288,384]{1,0:T(8,128)(2,1)} %wq_hbm.1, bf16[64,12288]{1,0:T(8,128)(2,1)} %bitcast.2, ...), custom_call_target="tpu_custom_call" | custom-call | flops 1207959552 | bytes 18874368 | tf_op jit(solution)/shard_map/pallas_call | solution.py:582
  56.0 1.5 %copy.12 = bf16[64,768]{1,0:T(8,128)(2,1)} copy(bf16[64,768]{1,0:T(8,128)(2,1)} %shard_map.100) | data formatting | bytes 196608

commit v2 on v1

--- a/solution.py
+++ b/solution.py
@@ -337,6 +337,9 @@
         ag_wait(last, h)
     project(last)
 
+    def q_copy(o, slot):
+        return remote(qsend.at[o], qbuf.at[slot], q_send.at[o], q_recv.at[slot], o)
+
     pk[...] = jnp.zeros_like(pk)
     q_all = accq[...]
     kv_all = q_all[:, qcols:qcols + kv_cols]
@@ -345,12 +348,12 @@
         for g in range(own_heads):
             pk[j, g * local_rows:(g + 1) * local_rows, :] = q_all[mine, g * HD:(g + 1) * HD]
         pk[j, own_heads * local_rows:tile, 0:kv_cols] = kv_all[mine, :]
-    qsend[...] = pk[...].astype(BF16)
-
-    def q_copy(o, slot):
-        return remote(qsend.at[o], qbuf.at[slot], q_send.at[o], q_recv.at[slot], o)
-
-    others(lambda o: q_copy(o, me).start())
+        qsend[j] = pk[j].astype(BF16)
+
+        @pl.when(j != me)
+        def _():
+            q_copy(j, me).start()
+
     qbuf[me] = qsend[me]
     def sent_gather(i, carry):
         pos, h = i // 2, i % 2
@@ -393,6 +396,9 @@
             part = part if p == 0 else pltpu.roll(part, p * kv_cols, 1)
             res = part if res is None else res + part
         return res
+
+    def a_copy(o, slot):
+        return remote(asend.at[o], abuf.at[slot], a_send.at[o], a_recv.at[slot], o)
 
     for k in range(KVH):
         at_k = slice(k * HD, (k + 1) * HD)
@@ -428,12 +434,13 @@
         summed = summed + own_weight.astype(BF16).astype(F32) * new_value
         result = (summed / total).astype(BF16)
         for s in range(per_head):
-            asend[k * per_head + s] = result[s * tile:(s + 1) * tile, :]
-
-    def a_copy(o, slot):
-        return remote(asend.at[o], abuf.at[slot], a_send.at[o], a_recv.at[slot], o)
-
-    others(lambda o: a_copy(o, me).start())
+            o = k * per_head + s
+            asend[o] = result[s * tile:(s + 1) * tile, :]
+
+            @pl.when(o != me)
+            def _():
+                a_copy(o, me).start()
+
     abuf[me] = asend[me]
     others(lambda o: q_copy(o, o).wait_send())
     for i in range(wo_parts):

time: 57.8 us -> 57.7 us (level)
  no operation moved by 1% of the time
where the time goes in v2:
time: 57.7 us; the launch traced here: 57.5 us
  Pallas kernels  55.9 us (97%)
  local copies, waits for them, and re-layouts  1.54 us (3%)
    pallas_call x1, Pallas kernels, fused_device(): pl.pallas_call(functools.partial(fused_kernel, n, rows, width, local_rows...  55.9 us
    unnamed x1, local copies, waits for them, and re-layouts  1.54 us

profile of v2, /device:TPU:0, one launch (start us, length us, event | category | flops | bytes accessed | tf_op | source)
XLA Modules:
  0.0 57.5 jit_solution(10196811461454843812)
XLA Ops:
  0.0 55.9 %shard_map.100 = bf16[64,768]{1,0:T(8,128)(2,1)} custom-call(s32[4]{0:T(128)} %len_ref.1, s32[4,4,4]{2,1,0:T(4,128)} %ks_ref.1, s32[4,4,4]{2,1,0:T(4,128)} %vs_ref.1, bf16[64,768]{1,0:T(8,128)(2,1)} %x_hbm.1, f32[1,12288]{1,0:T(1,128)} %bitcast.3, bf16[12288,384]{1,0:T(8,128)(2,1)} %wq_hbm.1, bf16[64,12288]{1,0:T(8,128)(2,1)} %bitcast.2, ...), custom_call_target="tpu_custom_call" | custom-call | flops 1207959552 | bytes 18874368 | tf_op jit(solution)/shard_map/pallas_call | solution.py:589
  56.0 1.5 %copy.12 = bf16[64,768]{1,0:T(8,128)(2,1)} copy(bf16[64,768]{1,0:T(8,128)(2,1)} %shard_map.100) | data formatting | bytes 196608

commit v3 on v0

--- a/solution.py
+++ b/solution.py
@@ -219,6 +219,7 @@
 
     def spread_line(pos, h):
         block = at(pos, b, c)
+        ag_copy(block, h, ag_y.at[2 * pos + h], ypeer).start()
 
         @pl.when((pos <= a) & (a < line - 1))
         def _():
@@ -228,15 +229,14 @@
         def _():
             ag_copy(block, h, ag_dn.at[2 * pos + h], down).start()
 
-        ag_copy(block, h, ag_y.at[2 * pos + h], ypeer).start()
         ag_copy(block, h, ag_core.at[2 * pos + h], cpeer).start()
 
     def ss_copy(o, slot):
         return remote(ssend, sbuf.at[slot], ss_send.at[o], ss_recv.at[slot], o)
 
-    others(lambda o: ss_copy(o, me).start())
     for h in range(2):
         spread_line(a, h)
+    others(lambda o: ss_copy(o, me).start())
     ridx = lax.broadcasted_iota(jnp.int32, (qrows, 128), 0) % local_rows
     pick = lax.broadcasted_iota(jnp.int32, (qrows, tile), 0) % local_rows
     pick = pick + own_heads * local_rows == lax.broadcasted_iota(jnp.int32, (qrows, tile), 1)

time: 57.3 us -> 58.9 us (1.028)
  Pallas kernels: 55.5 us -> 57.2 us
    pallas_call x1, Pallas kernels: 55.5 us -> 57.2 us  [fused_device(): pl.pallas_call(functools.partial(fused_kernel, n, rows, width, local_rows...]
where the time goes in v3:
time: 58.9 us; the launch traced here: 58.7 us
  Pallas kernels  57.2 us (97%)
  local copies, waits for them, and re-layouts  1.54 us (3%)
    pallas_call x1, Pallas kernels, fused_device(): pl.pallas_call(functools.partial(fused_kernel, n, rows, width, local_rows...  57.2 us
    unnamed x1, local copies, waits for them, and re-layouts  1.54 us

profile of v3, /device:TPU:0, one launch (start us, length us, event | category | flops | bytes accessed | tf_op | source)
XLA Modules:
  0.0 58.7 jit_solution(9704486439434485024)
XLA Ops:
  0.0 57.2 %shard_map.100 = bf16[64,768]{1,0:T(8,128)(2,1)} custom-call(s32[4]{0:T(128)} %len_ref.1, s32[4,4,4]{2,1,0:T(4,128)} %ks_ref.1, s32[4,4,4]{2,1,0:T(4,128)} %vs_ref.1, bf16[64,768]{1,0:T(8,128)(2,1)} %x_hbm.1, f32[1,12288]{1,0:T(1,128)} %bitcast.3, bf16[12288,384]{1,0:T(8,128)(2,1)} %wq_hbm.1, bf16[64,12288]{1,0:T(8,128)(2,1)} %bitcast.2, ...), custom_call_target="tpu_custom_call" | custom-call | flops 1207959552 | bytes 18874368 | tf_op jit(solution)/shard_map/pallas_call | solution.py:578
  57.2 1.5 %copy.12 = bf16[64,768]{1,0:T(8,128)(2,1)} copy(bf16[64,768]{1,0:T(8,128)(2,1)} %shard_map.100) | data formatting | bytes 196608
